TPU v7x, 256 devices: a whole 4x4x8 slice. The times are simulated.
256 devices in a mesh: dp: 64 (over x, z, core), clus: 4 (over y).
Axes of the slice: x: 4, y: 4, z: 8, core: 2. Of those that a mesh axis runs over, the one named last changes fastest.
Arguments:
- embeds: float32 [32768, 1024], P(('dp', 'clus')), may hold values from -300 to 300
- cluster_ids: int32 [32768], P(('dp', 'clus')), may hold values from 0 to 255, as said below
- inv_temp: float32 [256], P('dp'), may hold values from 40 to 400
Outputs:
- residual: float32 [32768, 1024], P(('dp', 'clus'))
- similarity: float32 [32768], P(('dp', 'clus'))
Inputs may be any that keep to these rules, and one draw needn't show every extreme that they name: `cluster_ids`: cluster c belongs to owner c // 4. Rows lie in aligned blocks of 128 rows, one block a device, in the order dp, clus. In every block at most 8 rows belong to clusters of one owner, and exactly 8 belong to one owner that is the same for all blocks of one index of clus. Every row shares its cluster with at least one other row of its block.
All inputs are finite; a program needn't handle non-finite values.
Results may differ from a plain program's by a relative error of at most 0.011.
Values may be sent and summed in bfloat16 or wider, within the bound.
A program may use at most 64 MiB of HBM per device.

v0:
```python
import jax
import jax.numpy as jnp
from jax import lax
from jax.sharding import PartitionSpec as P

lowest_score = -1e30


def absorb(running, key_rows, key_ids, key_tags, queries, query_ids, query_tags, query_temp):
    running_max, weight_total, summed = running
    cosine = lax.dot_general(
        queries, key_rows, (((1,), (1,)), ((), ())), preferred_element_type=jnp.float32
    )
    scores = query_temp[:, None] * cosine
    allowed = (
        (query_ids[:, None] == key_ids[None, :])
        & (query_ids[:, None] >= 0)
        & (query_tags[:, None] != key_tags[None, :])
    )
    new_max = jnp.maximum(running_max, jnp.max(jnp.where(allowed, scores, lowest_score), axis=1))
    weights = jnp.where(allowed, jnp.exp(scores - new_max[:, None]), 0.0)
    weight_total = jnp.sum(weights, axis=1)
    summed = jnp.dot(weights.astype(jnp.bfloat16), key_rows, preferred_element_type=jnp.float32)
    return (new_max, weight_total, summed)


def per_device(embeds, cluster_ids, inv_temp):
    row_count, feature_count = embeds.shape
    owners = lax.axis_size("dp")
    capacity = 4 * row_count // owners
    slots_all = owners * capacity
    per_owner = inv_temp.shape[0]
    unit_rows = embeds * lax.rsqrt(jnp.sum(embeds * embeds, axis=1, keepdims=True) + 1e-06)
    packed = unit_rows.astype(jnp.bfloat16)
    owner_of = cluster_ids // per_owner
    member = (owner_of[:, None] == jnp.arange(owners, dtype=jnp.int32)[None, :]).astype(jnp.int32)
    position = jnp.sum(jnp.cumsum(member, axis=0) * member, axis=1) - 1
    slot_index = owner_of * capacity + position
    my_column = lax.axis_index("clus")
    local_first = lax.axis_index("dp") * per_owner
    query_tags = my_column * slots_all + jnp.arange(slots_all, dtype=jnp.int32)
    initial = (
        jnp.full((slots_all,), lowest_score, jnp.float32),
        jnp.zeros((slots_all,), jnp.float32),
        jnp.zeros((slots_all, feature_count), jnp.float32),
    )
    send_rows = (
        jnp.zeros((slots_all, feature_count), jnp.bfloat16)
        .at[slot_index]
        .set(packed)
        .reshape(owners, capacity, feature_count)
    )
    send_ids = (
        jnp.full((slots_all,), -1, jnp.int32)
        .at[slot_index]
        .set(cluster_ids)
        .reshape(owners, capacity)
    )
    recv_rows, recv_ids = (
        lax.all_to_all(send_rows, "dp", split_axis=0, concat_axis=0, tiled=True),
        lax.all_to_all(send_ids, "dp", split_axis=0, concat_axis=0, tiled=True),
    )
    queries = recv_rows.reshape(slots_all, feature_count)
    query_ids = recv_ids.reshape(slots_all)
    local_ids = query_ids - local_first
    matches = local_ids[:, None] == jnp.arange(per_owner, dtype=jnp.int32)[None, :]
    found = jnp.sum(jnp.where(matches, inv_temp[None, :], 0.0), axis=1)
    query_temp = jnp.where(query_ids >= 0, found, 1.0)
    key_rows = lax.all_gather(queries, "clus", axis=0, tiled=True)
    key_ids = lax.all_gather(query_ids, "clus", axis=0, tiled=True)
    key_tags = jnp.arange(key_rows.shape[0], dtype=jnp.int32)
    running_max, weight_total, summed = absorb(
        initial, key_rows, key_ids, key_tags, queries, query_ids, query_tags, query_temp
    )
    neighbour = summed / jnp.where(weight_total > 0, weight_total, 1.0)[:, None]
    closest = jnp.where(query_ids >= 0, running_max / query_temp, 0.0)
    back_rows, back_close = (
        lax.all_to_all(
            neighbour.reshape(owners, capacity, feature_count).astype(jnp.bfloat16),
            "dp",
            split_axis=0,
            concat_axis=0,
            tiled=True,
        ).astype(jnp.float32),
        lax.all_to_all(
            closest.reshape(owners, capacity).astype(jnp.bfloat16),
            "dp",
            split_axis=0,
            concat_axis=0,
            tiled=True,
        ).astype(jnp.float32),
    )
    returned = back_rows.reshape(slots_all, feature_count)[slot_index]
    residual = unit_rows - returned
    similarity = back_close.reshape(slots_all)[slot_index]
    return (residual, similarity)


def solution(mesh):
    in_specs = (P(("dp", "clus"), None), P(("dp", "clus")), P("dp"))
    out_specs = (P(("dp", "clus"), None), P(("dp", "clus")))
    return jax.shard_map(
        per_device, mesh=mesh, in_specs=in_specs, out_specs=out_specs, check_vma=False
    )
```

profile of v0, /device:TPU:1, one launch (start us, length us, event | category | flops | bytes accessed | tf_op | source)
XLA Modules:
  0.0 181.4 jit_solution(6887126158780614839)
XLA Ops:
  7.2 0.0 copy-start.1
  7.2 0.0 all-gather.3.cloned.1.call-start
  7.2 0.7 and_select_fusion
  7.9 1.2 multiply_reduce_fusion
  9.1 0.1 fusion.16
  9.1 0.2 reduce_window_sum.11
  9.3 0.2 select_reduce_fusion.1
  9.5 0.7 compare_select_fusion.1
  10.2 2.0 %scatter_custom_fusion.1 = bf16[512,1024]{1,0:T(8,128)(2,1)S(1)} fusion(s32[128]{0:T(128)S(1)} %compare_select_fusion.1, bf16[]{:T(256)} %constant.53.clone.1, f32[128,1024]{1,0:T(8,128)} %param.3, f32[128]{0:T(128)S(1)} %add_rsqrt_fusion), kind=kCustom, calls=%fused_computation.17 | custom fusion | flops 262144 | bytes 1573378 | tf_op jit(solution)/shard_map/scatter | solution.py:50
  12.2 41.4 %all_to_all.25 = bf16[64,8,1024]{2,1,0:T(8,128)(2,1)} all-to-all(bf16[64,8,1024]{2,1,0:T(8,128)(2,1)S(1)} %bitcast.19), channel_id=1, replica_groups=mesh['dp'=64,'clus'=4] {'dp'}, dimensions={0} | all-to-all | bytes 2097152 | tf_op jit(solution)/shard_map/all_to_all | solution.py:60
  53.7 0.0 all-gather.3.cloned.1.call-update
  53.7 1.1 scatter_custom_fusion
  54.8 0.7 all_to_all.16
  55.5 6.2 %all-to-all-start = ((s32[64,1,8]{2,1,0:T(1,128)}), s32[64,1,8]{2,1,0:T(1,128)S(1)}, u32[]{:S(2)}, u32[]{:S(2)}) async-start(s32[64,1,8]{2,1,0:T(1,128)} %bitcast), calls=%async_computation | async-start | bytes 65536 | tf_op jit(solution)/shard_map/all_to_all | solution.py:61
  61.7 9.2 %all-to-all-done = s32[64,1,8]{2,1,0:T(1,128)S(1)} async-done(((s32[64,1,8]{2,1,0:T(1,128)}), s32[64,1,8]{2,1,0:T(1,128)S(1)}, u32[]{:S(2)}, u32[]{:S(2)}) %all-to-all-start) | async-done | bytes 2080 | tf_op jit(solution)/shard_map/all_to_all | solution.py:61
  70.9 0.1 reshape.132
  71.0 0.5 broadcast.102
  71.5 0.7 reduce.9
  72.3 0.1 eq.44
  72.4 0.0 copy-done.1
  72.4 0.1 select_reduce_fusion.2
  72.5 0.1 reduce_sum.42
  72.6 0.1 copy.13
  72.6 0.1 copy.12
  72.7 9.7 %all-gather = s32[4,1,512]{2,1,0:T(1,128)S(1)} all-gather(s32[1,1,512]{2,1,0:T(1,128)S(1)} %reshape.132), channel_id=1, replica_groups=mesh['dp'=64,'clus'=4] {'clus'}, dimensions={0}, use_global_device_ids=true | all-gather | bytes 10240 | tf_op jit(solution)/shard_map/all_gather | solution.py:70
  82.3 19.5 %all-gather.3.cloned.1.call-done = bf16[2048,1024]{1,0:T(8,128)(2,1)} async-done(((bf16[512,1024]{1,0:T(8,128)(2,1)}), bf16[2048,1024]{1,0:T(8,128)(2,1)}) %all-gather.3.cloned.1.call-update) | async-done | bytes 4194320 | tf_op jit(solution)/shard_map/all_gather | solution.py:69
  101.8 7.3 %select_reduce_fusion = (f32[512]{0:T(512)S(1)}, f32[512,2048]{1,0:T(8,128)}) fusion(f32[512]{0:T(512)S(1)} %get-tuple-element.2, s32[512]{0:T(512)S(1)} %iota_add_fusion, pred[512]{0:T(512)(128)(4,1)S(1)} %get-tuple-element.3, s32[2048]{0:T(1024)S(1)} %bitcast.21, s32[512]{0:T(512)S(1)} %eq.44, bf16[2048,1024]{1,0:T(8,128)(2,1)} %all-gather.3.cloned.1.call-done, ...), kind=kOutput, calls=%fused_computation.5 | convolution fusion | flops 2154823168 | bytes 9454080 | tf_op jit(solution)/shard_map/dot_general | solution.py:11
  109.2 0.1 max_broadcast_in_dim.19
  109.3 3.8 %fusion.1 = f32[512]{0:T(512)S(1)} fusion(f32[512,2048]{1,0:T(8,128)} %get-tuple-element.5, f32[512]{0:T(512)S(1)} %broadcast_maximum_fusion, f32[512]{0:T(512)S(1)} %get-tuple-element.2, s32[512]{0:T(512)S(1)} %iota_add_fusion, pred[512]{0:T(512)(128)(4,1)S(1)} %get-tuple-element.3, s32[2048]{0:T(1024)S(1)} %bitcast.22, s32[512]{0:T(512)S(1)} %eq.44), kind=kLoop, calls=%fused_computation.8 | loop fusion | flops 8388096 | bytes 4213248 | tf_op jit(solution)/shard_map/reduce_sum | solution.py:22
  113.1 0.1 copy.14
  113.2 0.7 copy.15
  113.9 10.6 %all-to-all-start.3 = ((bf16[64,1,8]{2,1,0:T(2,128)(2,1)}), bf16[64,1,8]{2,1,0:T(2,128)(2,1)S(1)}, u32[]{:S(2)}, u32[]{:S(2)}) async-start(bf16[64,1,8]{2,1,0:T(2,128)(2,1)} %copy.15), calls=%async_computation.3 | async-start | bytes 65536 | tf_op jit(solution)/shard_map/all_to_all | solution.py:85
  124.6 7.8 %fusion.10 = bf16[64,8,1024]{2,1,0:T(8,128)(2,1)} fusion(bf16[2048,1024]{1,0:T(8,128)(2,1)} %all-gather.3.cloned.1.call-done, f32[512,2048]{1,0:T(8,128)} %get-tuple-element.5, f32[512]{0:T(512)S(1)} %broadcast_maximum_fusion, f32[512]{0:T(512)S(1)} %get-tuple-element.2, f32[512]{0:T(512)S(1)} %compare_select_fusion, s32[512]{0:T(512)S(1)} %iota_add_fusion, ...), kind=kOutput, calls=%fused_computation.15 | convolution fusion | flops 2156920832 | bytes 9456128 | tf_op jit(solution)/shard_map/dot_general | solution.py:23
  132.4 1.4 all-to-all-done.3
  133.8 9.1 %all-to-all-start.2 = ((bf16[64,8,1024]{2,1,0:T(8,128)(2,1)}), bf16[64,8,1024]{2,1,0:T(8,128)(2,1)}, u32[]{:S(2)}, u32[]{:S(2)}) async-start(bf16[64,8,1024]{2,1,0:T(8,128)(2,1)} %fusion.10), calls=%async_computation.2 | async-start | bytes 2097152 | tf_op jit(solution)/shard_map/all_to_all | solution.py:78
  142.9 0.1 convert_reduce_fusion
  143.0 0.1 reshape.95
  143.1 0.0 copy-start
  143.1 1.8 gather_fusion.1
  144.9 26.5 %all-to-all-done.2 = bf16[64,8,1024]{2,1,0:T(8,128)(2,1)} async-done(((bf16[64,8,1024]{2,1,0:T(8,128)(2,1)}), bf16[64,8,1024]{2,1,0:T(8,128)(2,1)}, u32[]{:S(2)}, u32[]{:S(2)}) %all-to-all-start.2) | async-done | bytes 1048608 | tf_op jit(solution)/shard_map/all_to_all | solution.py:78
  171.4 1.5 bitcast_convert_fusion
  172.8 0.8 gather_fusion
  173.6 0.0 copy-done
  173.6 0.9 multiply_subtract_fusion
  (8 shorter events, 0.0 us)
Async XLA Ops:
  7.2 65.2 %copy-start.1 = (f32[4]{0:T(128)S(1)}, f32[4]{0:T(128)}, u32[]{:S(2)}) copy-start(f32[4]{0:T(128)} %param.5) | copy-start | bytes 52
  7.2 94.7 %all-gather.3.cloned.1.call-start = ((), (), s32[]{:S(2)}) async-start(), calls=%async_computation.4 | async-start | bytes 5242880 | tf_op jit(solution)/shard_map/all_gather | solution.py:69
  55.5 15.4 %all-to-all-start = ((s32[64,1,8]{2,1,0:T(1,128)}), s32[64,1,8]{2,1,0:T(1,128)S(1)}, u32[]{:S(2)}, u32[]{:S(2)}) async-start(s32[64,1,8]{2,1,0:T(1,128)} %bitcast), calls=%async_computation | async-start | bytes 65536 | tf_op jit(solution)/shard_map/all_to_all | solution.py:61
  113.9 19.9 %all-to-all-start.3 = ((bf16[64,1,8]{2,1,0:T(2,128)(2,1)}), bf16[64,1,8]{2,1,0:T(2,128)(2,1)S(1)}, u32[]{:S(2)}, u32[]{:S(2)}) async-start(bf16[64,1,8]{2,1,0:T(2,128)(2,1)} %copy.15), calls=%async_computation.3 | async-start | bytes 65536 | tf_op jit(solution)/shard_map/all_to_all | solution.py:85
  133.8 37.6 %all-to-all-start.2 = ((bf16[64,8,1024]{2,1,0:T(8,128)(2,1)}), bf16[64,8,1024]{2,1,0:T(8,128)(2,1)}, u32[]{:S(2)}, u32[]{:S(2)}) async-start(bf16[64,8,1024]{2,1,0:T(8,128)(2,1)} %fusion.10), calls=%async_computation.2 | async-start | bytes 2097152 | tf_op jit(solution)/shard_map/all_to_all | solution.py:78
  143.1 30.5 %copy-start = (f32[128,1024]{1,0:T(8,128)S(1)}, f32[128,1024]{1,0:T(8,128)}, u32[]{:S(2)}) copy-start(f32[128,1024]{1,0:T(8,128)} %param.3) | copy-start | bytes 1572868
Sparse Core Ops, SparseCore 0:
  53.8 47.9 all-gather.2
where the time goes:
time: 182 us; the launch traced here: 181 us
  waiting for transfers between devices  56.6 us (31%)
  blocking collectives  51.1 us (28%)
  starting transfers between devices  26 us (14%)
  matrix products  15.1 us (8%)
  between operations  14.2 us (8%)
  other arithmetic  12.1 us (7%)
  local copies, waits for them, and re-layouts  6.26 us (3%)
    all_to_all x1, blocking collectives, per_device(): lax.all_to_all(send_rows, 'dp', split_axis=0, concat_axis=0, tiled=True)  41.4 us
    all_to_all x1, waiting for transfers between devices, per_device(): lax.all_to_all(neighbour.reshape(owners, capacity, feature_count).astype(...  26.5 us
    all_gather x1, waiting for transfers between devices, per_device(): key_rows = lax.all_gather(queries, 'clus', axis=0, tiled=True)  19.5 us
    all_to_all x1, starting transfers between devices, per_device(): lax.all_to_all(closest.reshape(owners, capacity).astype(jnp.bfloat16), 'd...  10.6 us
    all_gather x1, blocking collectives, per_device(): key_ids = lax.all_gather(query_ids, 'clus', axis=0, tiled=True)  9.66 us
    all_to_all x1, waiting for transfers between devices, per_device(): lax.all_to_all(send_ids, 'dp', split_axis=0, concat_axis=0, tiled=True)  9.19 us
    all_to_all x1, starting transfers between devices, per_device(): lax.all_to_all(neighbour.reshape(owners, capacity, feature_count).astype(...  9.09 us
    dot_general x1, matrix products, absorb(): jnp.dot(weights.astype(jnp.bfloat16), key_rows, preferred_element_type=jn...  7.79 us
  transfers between devices with their start and end apart: 4, of which 4 were waited for; matrix products, arithmetic and copies ran while one was open for 7% of the time, Pallas kernels for 0%

commit v1 on v0

v1 whole, which is shorter than its diff:
```python
import functools

import jax
import jax.numpy as jnp
from jax import lax
from jax.experimental import pallas as pl
from jax.experimental.pallas import tpu as pltpu
from jax.sharding import PartitionSpec as P

NX, NZ, NC, NY = 4, 8, 2, 4
CAP = 8
LOWEST = -1e30
MESH = pl.DeviceIdType.MESH
F32 = jnp.float32
BF16 = jnp.bfloat16


def wait_bytes(ref, sem):
    pltpu.make_async_copy(ref, ref, sem).wait()


def kernel(
    ids_ref, x_ref, temp_ref, out_ref, sim_ref,
    unit, halves, send, keys, table, scores, weights, outs, back, turned,
    id_send, id_recv, key_ids, sim_send, sim_recv,
    row_send_sem, row_recv_sem, right_send_sem, left_send_sem, relay_send_sem,
    y_recv_sem, far_recv_sem, id_send_sem, id_recv_sem, kid_send_sem, kid_recv_sem,
    back_send_sem, back_recv_sem, sim_send_sem, sim_recv_sem,
):
    group = NX * NC
    owners = group * NZ
    rows, width = x_ref.shape
    half = width // 2
    slots = owners * CAP
    per_owner = temp_ref.shape[0]
    chunk_rows = group * CAP

    me = lax.axis_index("dp")
    my_y = lax.axis_index("clus")
    my_c = lax.rem(me, NC)
    my_z = lax.rem(lax.div(me, NC), NZ)
    my_x = lax.div(me, NC * NZ)
    y_right = lax.rem(my_y + 1, NY)
    y_left = lax.rem(my_y + NY - 1, NY)
    y_far = lax.rem(my_y + 2, NY)

    def shift_of(k):
        m = lax.div(k, group)
        g = lax.rem(k, group)
        odd = lax.rem(m, 2)
        dz = odd * lax.div(m + 1, 2) + (1 - odd) * lax.rem(NZ - lax.div(m, 2), NZ)
        return lax.div(g, NC), dz, lax.rem(g, NC)

    def ahead(k):
        dx, dz, dc = shift_of(k)
        x, z, c = lax.rem(my_x + dx, NX), lax.rem(my_z + dz, NZ), lax.rem(my_c + dc, NC)
        return (x * NZ + z) * NC + c

    def behind(k):
        dx, dz, dc = shift_of(k)
        x, z, c = lax.rem(my_x + NX - dx, NX), lax.rem(my_z + NZ - dz, NZ), lax.rem(my_c + NC - dc, NC)
        return (x * NZ + z) * NC + c

    barrier = pltpu.get_barrier_semaphore()

    @pl.loop(1, owners)
    def _(k):
        pl.semaphore_signal(barrier, inc=1, device_id=(ahead(k), my_y), device_id_type=MESH)

    for y in (y_right, y_left, y_far):
        pl.semaphore_signal(barrier, inc=1, device_id=(me, y), device_id_type=MESH)

    x = x_ref[...]
    unit_rows = x * lax.rsqrt(jnp.sum(x * x, axis=1, keepdims=True) + 1e-06)
    unit[...] = unit_rows
    packed = unit_rows.astype(BF16)
    halves[:rows, :] = packed[:, :half]
    halves[rows:, :] = packed[:, half:]

    ids = ids_ref[...]
    owner = lax.div(ids, per_owner)
    local = lax.rem(ids, per_owner)
    dx = lax.rem(lax.div(owner, NC * NZ) - my_x + NX, NX)
    dz = lax.rem(lax.rem(lax.div(owner, NC), NZ) - my_z + NZ, NZ)
    dc = lax.rem(lax.rem(owner, NC) - my_c + NC, NC)
    place = jnp.where(dz == 0, 0, jnp.where(dz <= NZ // 2, 2 * dz - 1, 2 * (NZ - dz)))
    offset = place * group + dx * NC + dc
    offset_f = jnp.broadcast_to(offset.astype(F32), (rows, rows))
    same = offset_f == offset_f.T
    earlier = lax.broadcasted_iota(jnp.int32, (rows, rows), 0) < lax.broadcasted_iota(jnp.int32, (rows, rows), 1)
    rank = jnp.sum(jnp.where(same & earlier, 1.0, 0.0), axis=0, keepdims=True).astype(jnp.int32)
    target = offset * (2 * CAP) + rank
    targets = jnp.concatenate([target, target + CAP], axis=1)

    at_offset = lax.broadcasted_iota(jnp.int32, (owners, rows), 0) == offset
    at_rank = lax.broadcasted_iota(jnp.int32, (128, rows), 0) == rank
    id_table = lax.dot_general(
        jnp.where(at_offset, 1.0, 0.0).astype(BF16),
        jnp.where(at_rank, (local + 1).astype(F32), 0.0).astype(BF16),
        (((1,), (1,)), ((), ())),
        preferred_element_type=F32,
    ) - 1.0
    for k in range(owners):
        id_send[k] = id_table[k : k + 1, :]
    id_recv[0] = id_table[0:1, :]

    pl.semaphore_wait(barrier, owners - 1 + NY - 1)

    slab = group * 2 * CAP

    for m in range(NZ):
        hit = lax.broadcasted_iota(jnp.int32, (slab, 2 * rows), 0) + m * slab == targets
        part = jnp.dot(jnp.where(hit, 1.0, 0.0).astype(BF16), halves[...], preferred_element_type=F32)
        send[m * group : (m + 1) * group] = part.astype(BF16).reshape(group, 2 * CAP, half)
        if m == 0:
            keys[0, 0] = send[0]

        @pl.loop(max(m * group, 1), (m + 1) * group)
        def _(k):
            pltpu.make_async_remote_copy(
                src_ref=send.at[k], dst_ref=keys.at[0, k],
                send_sem=row_send_sem, recv_sem=row_recv_sem.at[m],
                device_id=(ahead(k), my_y), device_id_type=MESH,
            ).start()

    @pl.loop(1, owners)
    def _(k):
        pltpu.make_async_remote_copy(
            src_ref=id_send.at[k], dst_ref=id_recv.at[k],
            send_sem=id_send_sem, recv_sem=id_recv_sem,
            device_id=(ahead(k), my_y), device_id_type=MESH,
        ).start()

    strip = min(128, owners * 2 * CAP)
    targets_f = jnp.broadcast_to(targets.astype(F32), (strip, 2 * rows)).T
    lanes = lax.broadcasted_iota(jnp.int32, (2 * rows, strip), 1).astype(F32)
    for j in range(owners * 2 * CAP // strip):
        turned[:, j * strip : (j + 1) * strip] = jnp.where(lanes + j * strip == targets_f, 1.0, 0.0).astype(BF16)

    def unpack(column, m):
        part = keys[column, m * group : (m + 1) * group].astype(F32)
        first = column * slots + m * chunk_rows
        table[first : first + chunk_rows, :half] = part[:, :CAP, :].reshape(chunk_rows, half).astype(BF16)
        table[first : first + chunk_rows, half:] = part[:, CAP:, :].reshape(chunk_rows, half).astype(BF16)

    def chunk(column, m):
        return keys.at[column, pl.ds(m * group, group)]

    def relay(m):
        wait_bytes(chunk(1, m), y_recv_sem.at[0, m])
        wait_bytes(chunk(3, m), y_recv_sem.at[1, m])
        source, to = (1, y_right) if m % 2 == 0 else (3, y_left)
        pltpu.make_async_remote_copy(
            src_ref=chunk(source, m), dst_ref=chunk(2, m),
            send_sem=relay_send_sem, recv_sem=far_recv_sem.at[m],
            device_id=(me, to), device_id_type=MESH,
        ).start()
        unpack(1, m)
        unpack(3, m)

    for m in range(NZ):
        arriving = keys.at[0, pl.ds(1, group - 1)] if m == 0 else chunk(0, m)
        wait_bytes(arriving, row_recv_sem.at[m])
        for way, to, column, sem in ((0, y_right, 1, right_send_sem), (1, y_left, 3, left_send_sem)):
            pltpu.make_async_remote_copy(
                src_ref=chunk(0, m), dst_ref=chunk(column, m),
                send_sem=sem, recv_sem=y_recv_sem.at[way, m],
                device_id=(me, to), device_id_type=MESH,
            ).start()
        unpack(0, m)
        if m == 1:
            wait_bytes(id_recv.at[pl.ds(1, owners - 1)], id_recv_sem)
            got = jnp.concatenate([id_recv[k] for k in range(owners)], axis=0)
            spread = (
                lax.broadcasted_iota(jnp.int32, (128, slots), 0)
                == lax.rem(lax.broadcasted_iota(jnp.int32, (128, slots), 1), CAP)
            )
            wide = jnp.dot(got.astype(BF16), jnp.where(spread, 1.0, 0.0).astype(BF16), preferred_element_type=F32)
            own = (
                lax.broadcasted_iota(jnp.int32, (owners, slots), 0)
                == lax.div(lax.broadcasted_iota(jnp.int32, (owners, slots), 1), CAP)
            )
            key_ids[0] = jnp.sum(jnp.where(own, wide, 0.0), axis=0, keepdims=True)
            for n, (to, column) in enumerate(((y_right, 1), (y_left, 3), (y_far, 2))):
                pltpu.make_async_remote_copy(
                    src_ref=key_ids.at[0], dst_ref=key_ids.at[column],
                    send_sem=kid_send_sem.at[n], recv_sem=kid_recv_sem.at[n],
                    device_id=(me, to), device_id_type=MESH,
                ).start()
        if m >= 1:
            relay(m - 1)
    relay(NZ - 1)

    for n, column in enumerate((1, 3, 2)):
        wait_bytes(key_ids.at[column], kid_recv_sem.at[n])

    query_id = jnp.broadcast_to(key_ids[0], (128, slots)).T[:, 0:1]
    query_temp = jnp.ones_like(query_id)
    for c in range(per_owner):
        query_temp = jnp.where(query_id == float(c), temp_ref[c], query_temp)
    query_id = jnp.where(query_id < 0.0, -2.0, query_id)

    block = min(256, slots)
    best = [jnp.full((block, 1), LOWEST, F32) for _ in range(slots // block)]
    for column in (0, 1, 3, 2):
        if column == 2:
            for m in range(NZ):
                wait_bytes(chunk(2, m), far_recv_sem.at[m])
                unpack(2, m)
        for b in range(slots // block):
            cosine = lax.dot_general(
                table[b * block : (b + 1) * block, :],
                table[column * slots : (column + 1) * slots, :],
                (((1,), (1,)), ((), ())),
                preferred_element_type=F32,
            )
            allowed = query_id[b * block : (b + 1) * block] == key_ids[column]
            if column == 0:
                allowed &= (
                    lax.broadcasted_iota(jnp.int32, (block, slots), 0) + b * block
                    != lax.broadcasted_iota(jnp.int32, (block, slots), 1)
                )
            score = jnp.where(allowed, cosine * query_temp[b * block : (b + 1) * block], LOWEST)
            scores[b * block : (b + 1) * block, column * slots : (column + 1) * slots] = score
            best[b] = jnp.maximum(best[b], jnp.max(score, axis=1, keepdims=True))

    per_block = block // CAP
    for b in range(slots // block - 1, -1, -1):
        here = pl.ds(b * block, block)
        close = best[b] / query_temp[b * block : (b + 1) * block]
        lane = lax.broadcasted_iota(jnp.int32, (block, 128), 1)
        rank_of = lax.rem(lax.broadcasted_iota(jnp.int32, (block, 128), 0), CAP)
        spread_close = jnp.sum(jnp.where(lane == rank_of, close, 0.0).reshape(per_block, CAP, 128), axis=1)
        for k in range(per_block):
            sim_send[b * per_block + k] = spread_close[k : k + 1, :]
        total = jnp.zeros((block, 1), F32)
        for column in range(NY):
            weight = jnp.exp(scores[here, column * slots : (column + 1) * slots] - best[b])
            total += jnp.sum(weight, axis=1, keepdims=True)
            weights[:, column * slots : (column + 1) * slots] = weight.astype(BF16)
        for h in range(2):
            summed = jnp.dot(weights[...], table[:, h * half : (h + 1) * half], preferred_element_type=F32)
            near = (summed / total).reshape(per_block, CAP, half)
            if h == 0:
                left = near
        outs[pl.ds(b * per_block, per_block)] = jnp.concatenate([left, near], axis=1).astype(BF16)
        if b == 0:
            back[0] = outs[0]
            sim_recv[0] = sim_send[0]

        @pl.loop(max(b * per_block, 1), (b + 1) * per_block)
        def _(k):
            to = behind(k)
            pltpu.make_async_remote_copy(
                src_ref=outs.at[k], dst_ref=back.at[k],
                send_sem=back_send_sem, recv_sem=back_recv_sem,
                device_id=(to, my_y), device_id_type=MESH,
            ).start()
            pltpu.make_async_remote_copy(
                src_ref=sim_send.at[k], dst_ref=sim_recv.at[k],
                send_sem=sim_send_sem, recv_sem=sim_recv_sem,
                device_id=(to, my_y), device_id_type=MESH,
            ).start()

    others = pl.ds(1, owners - 1)
    wait_bytes(sim_recv.at[others], sim_recv_sem)
    got = jnp.concatenate([sim_recv[k] for k in range(owners)], axis=0)
    picked = lax.dot_general(
        got, jnp.where(at_offset, 1.0, 0.0), (((0,), (0,)), ((), ())),
        preferred_element_type=F32, precision=lax.Precision.HIGHEST,
    )
    sim_ref[...] = jnp.sum(jnp.where(at_rank, picked, 0.0), axis=0, keepdims=True)

    wait_bytes(back.at[others], back_recv_sem)
    returned = jnp.dot(
        turned[...], back[...].reshape(owners * 2 * CAP, half), preferred_element_type=F32
    )
    out_ref[:, :half] = unit[:, :half] - returned[:rows]
    out_ref[:, half:] = unit[:, half:] - returned[rows:]

    wait_bytes(send.at[others], row_send_sem)
    wait_bytes(id_send.at[others], id_send_sem)
    wait_bytes(outs.at[others], back_send_sem)
    wait_bytes(sim_send.at[others], sim_send_sem)
    wait_bytes(keys.at[0], right_send_sem)
    wait_bytes(keys.at[0], left_send_sem)
    wait_bytes(keys.at[2], relay_send_sem)
    for n in range(3):
        wait_bytes(key_ids.at[0], kid_send_sem.at[n])


def per_device(embeds, cluster_ids, inv_temp):
    rows, width = embeds.shape
    group = NX * NC
    owners = group * NZ
    slots = owners * CAP
    half = width // 2
    block = min(256, slots)
    DMA = pltpu.SemaphoreType.DMA
    vmem = pl.BlockSpec(memory_space=pltpu.VMEM)
    residual, similarity = pl.pallas_call(
        kernel,
        out_shape=(jax.ShapeDtypeStruct((rows, width), F32), jax.ShapeDtypeStruct((1, rows), F32)),
        in_specs=[vmem, vmem, pl.BlockSpec(memory_space=pltpu.SMEM)],
        out_specs=(vmem, vmem),
        scratch_shapes=[
            pltpu.VMEM((rows, width), F32),
            pltpu.VMEM((2 * rows, half), BF16),
            pltpu.VMEM((owners, 2 * CAP, half), BF16),
            pltpu.VMEM((NY, owners, 2 * CAP, half), BF16),
            pltpu.VMEM((NY * slots, width), BF16),
            pltpu.VMEM((slots, NY * slots), F32),
            pltpu.VMEM((block, NY * slots), BF16),
            pltpu.VMEM((owners, 2 * CAP, half), BF16),
            pltpu.VMEM((owners, 2 * CAP, half), BF16),
            pltpu.VMEM((2 * rows, owners * 2 * CAP), BF16),
            pltpu.VMEM((owners, 1, 128), F32),
            pltpu.VMEM((owners, 1, 128), F32),
            pltpu.VMEM((NY, 1, slots), F32),
            pltpu.VMEM((owners, 1, 128), F32),
            pltpu.VMEM((owners, 1, 128), F32),
            DMA, DMA((NZ,)), DMA, DMA, DMA,
            DMA((2, NZ)), DMA((NZ,)), DMA, DMA, DMA((3,)), DMA((3,)),
            DMA, DMA, DMA, DMA,
        ],
        compiler_params=pltpu.CompilerParams(
            collective_id=0, has_side_effects=True, vmem_limit_bytes=48 * 1024 * 1024
        ),
    )(cluster_ids.reshape(1, rows), embeds, inv_temp)
    return residual, similarity.reshape(rows)


def solution(mesh):
    in_specs = (P(("dp", "clus"), None), P(("dp", "clus")), P("dp"))
    out_specs = (P(("dp", "clus"), None), P(("dp", "clus")))
    return jax.shard_map(
        per_device, mesh=mesh, in_specs=in_specs, out_specs=out_specs, check_vma=False
    )
```

time: 182 us -> 108 us (0.59)
  Pallas kernels: 0 us -> 104 us
  waiting for transfers between devices: 56.6 us -> 0 us
  blocking collectives: 51.1 us -> 0 us
  starting transfers between devices: 26 us -> 0 us
  matrix products: 15.1 us -> 0 us
  between operations: 14.2 us -> 0.66 us
  other arithmetic: 12.1 us -> 0 us
  local copies, waits for them, and re-layouts: 6.26 us -> 3 us
    pallas_call x0 -> x1, Pallas kernels: none -> 104 us  [per_device(): pl.pallas_call(kernel, out_shape=(jax.ShapeDtypeStruct((rows, width), F32...]
    all_to_all x1 -> x0, blocking collectives: 41.4 us -> none  [per_device(): lax.all_to_all(send_rows, 'dp', split_axis=0, concat_axis=0, tiled=True)]
    all_to_all x3 -> x0, waiting for transfers between devices: 37.1 us -> none  [the longest x1 26.5 us: per_device(): lax.all_to_all(neighbour.reshape(owners, capacity, feature_count).astype(...]
    all_to_all x3 -> x0, starting transfers between devices: 25.9 us -> none  [the longest x1 10.6 us: per_device(): lax.all_to_all(closest.reshape(owners, capacity).astype(jnp.bfloat16), 'd...]
    all_gather x1 -> x0, waiting for transfers between devices: 19.5 us -> none  [per_device(): key_rows = lax.all_gather(queries, 'clus', axis=0, tiled=True)]
    dot_general x2 -> x0, matrix products: 15.1 us -> none  [the longest x1 7.79 us: absorb(): jnp.dot(weights.astype(jnp.bfloat16), key_rows, preferred_element_type=jn...]
    all_gather x1 -> x0, blocking collectives: 9.66 us -> none  [per_device(): key_ids = lax.all_gather(query_ids, 'clus', axis=0, tiled=True)]
    reduce_sum x4 -> x0, other arithmetic: 5.23 us -> none  [the longest x1 3.82 us: absorb(): weight_total = jnp.sum(weights, axis=1)]
  transfers between devices with their start and end apart: 4 -> 0, of which waited for: 4 -> 0; matrix products, arithmetic and copies ran while one was open for 7% -> 0% of each run, Pallas kernels for 0% -> 0%
where the time goes in v1:
time: 108 us; the launch traced here: 107 us
  Pallas kernels  104 us (96%)
  local copies, waits for them, and re-layouts  3 us (3%)
    pallas_call x1, Pallas kernels, per_device(): pl.pallas_call(kernel, out_shape=(jax.ShapeDtypeStruct((rows, width), F32...  104 us
    unnamed x8, local copies, waits for them, and re-layouts  3 us

profile of v1, /device:TPU:1, one launch (start us, length us, event | category | flops | bytes accessed | tf_op | source)
XLA Modules:
  0.0 107.4 jit_solution(17285914696919992418)
XLA Ops:
  0.6 0.0 copy-start.2
  0.6 0.0 copy-start.1
  0.6 0.6 copy-done.2
  1.3 0.0 copy-done.1
  1.3 0.0 copy-start
  1.3 1.0 copy-done
  2.3 103.8 %shard_map.50 = (f32[128,1024]{1,0:T(8,128)S(1)}, f32[1,128]{1,0:T(1,128)S(1)}) custom-call(s32[1,128]{1,0:T(1,128)S(1)} %bitcast.2, f32[128,1024]{1,0:T(8,128)S(1)} %copy-done, f32[4]{0:T(128)S(1)} %copy-done.2), custom_call_target="tpu_custom_call" | custom-call | tf_op jit(solution)/shard_map/pallas_call | solution.py:301
  106.1 0.8 copy.7
  106.9 0.5 copy.8
Async XLA Ops:
  0.6 0.7 copy-start.2
  0.6 0.7 copy-start.1
  1.3 1.0 copy-start

commit v2 on v1

v2 whole, which is shorter than its diff:
```python
import functools

import jax
import jax.numpy as jnp
from jax import lax
from jax.experimental import pallas as pl
from jax.experimental.pallas import tpu as pltpu
from jax.sharding import PartitionSpec as P

NX, NZ, NC, NY = 4, 8, 2, 4
CAP = 8
LOWEST = -1e30
AHEAD = 4
MESH = pl.DeviceIdType.MESH
F32 = jnp.float32
BF16 = jnp.bfloat16


def wait_bytes(ref, sem):
    pltpu.make_async_copy(ref, ref, sem).wait()


def kernel(
    ids_hbm, x_hbm, temp_ref, out_ref, sim_ref,
    ids_ref, x_ref, unit, halves, send, keys, table, scores, weights, outs, back, turned,
    raw, key_ids, sim_send, sim_mid, sim_recv,
    load_sem, ready_sem, row_send_sem, row_recv_sem, y_send_sem, relay_send_sem,
    y_recv_sem, far_recv_sem, raw_send_sem, raw_z_sem, raw_plane_sem, raw_y_sem,
    back_send_sem, back_recv_sem, sim_send_sem, sim_z_sem, sim_plane_sem,
):
    group = NX * NC
    owners = group * NZ
    rows, width = x_ref.shape
    half = width // 2
    slots = owners * CAP
    per_owner = temp_ref.shape[0]
    chunk_rows = group * CAP
    near_group = group // 2

    me = lax.axis_index("dp")
    my_y = lax.axis_index("clus")
    my_c = lax.rem(me, NC)
    my_z = lax.rem(lax.div(me, NC), NZ)
    my_x = lax.div(me, NC * NZ)
    y_right = lax.rem(my_y + 1, NY)
    y_left = lax.rem(my_y + NY - 1, NY)
    y_far = lax.rem(my_y + 2, NY)

    def swap(m):
        return m if m == 0 or m == NZ - 1 else (m + 1 if m % 2 else m - 1)

    def shift_of(m, g):
        far = lax.div(m + 1, 2)
        odd = lax.rem(m + lax.div(g, near_group), 2)
        dz = odd * far + (1 - odd) * lax.rem(NZ - far, NZ)
        return lax.div(g, NC), dz, lax.rem(g, NC)

    def ahead(m, g):
        dx, dz, dc = shift_of(m, g)
        x, z, c = lax.rem(my_x + dx, NX), lax.rem(my_z + dz, NZ), lax.rem(my_c + dc, NC)
        return ((x * NZ + z) * NC + c, my_y)

    def behind(m, g):
        dx, dz, dc = shift_of(m, g)
        x, z, c = lax.rem(my_x + NX - dx, NX), lax.rem(my_z + NZ - dz, NZ), lax.rem(my_c + NC - dc, NC)
        return ((x * NZ + z) * NC + c, my_y)

    def plane(g):
        x, c = lax.rem(my_x + lax.div(g, NC), NX), lax.rem(my_c + lax.rem(g, NC), NC)
        return ((x * NZ + my_z) * NC + c, my_y)

    def plane_back(g):
        x, c = lax.rem(my_x + NX - lax.div(g, NC), NX), lax.rem(my_c + NC - lax.rem(g, NC), NC)
        return ((x * NZ + my_z) * NC + c, my_y)

    def push(src, dst, send_sem, recv_sem, to):
        pltpu.make_async_remote_copy(
            src_ref=src, dst_ref=dst, send_sem=send_sem, recv_sem=recv_sem,
            device_id=to, device_id_type=MESH,
        ).start()

    loads = [
        pltpu.make_async_copy(x_hbm, x_ref, load_sem.at[0]),
        pltpu.make_async_copy(ids_hbm, ids_ref, load_sem.at[1]),
    ]
    for load in loads:
        load.start()

    barrier = pltpu.get_barrier_semaphore()

    @pl.loop(1, group)
    def _(g):
        pl.semaphore_signal(barrier, inc=1, device_id=plane(g), device_id_type=MESH)

    @pl.loop(1, NZ)
    def _(m):
        pl.semaphore_signal(barrier, inc=1, device_id=ahead(m, 0), device_id_type=MESH)

    for y in (y_right, y_left, y_far):
        pl.semaphore_signal(barrier, inc=1, device_id=(me, y), device_id_type=MESH)

    loads[1].wait()
    loads[0].wait()
    x = x_ref[...]
    unit_rows = x * lax.rsqrt(jnp.sum(x * x, axis=1, keepdims=True) + 1e-06)
    unit[...] = unit_rows
    packed = unit_rows.astype(BF16)
    halves[:rows, :] = packed[:, :half]
    halves[rows:, :] = packed[:, half:]

    ids = ids_ref[...]
    owner = lax.div(ids, per_owner)
    dx = lax.rem(lax.div(owner, NC * NZ) - my_x + NX, NX)
    dz = lax.rem(lax.rem(lax.div(owner, NC), NZ) - my_z + NZ, NZ)
    dc = lax.rem(lax.rem(owner, NC) - my_c + NC, NC)
    g_of = dx * NC + dc
    up = jnp.where(g_of < near_group, 2 * dz - 1, 2 * dz)
    down = jnp.where(g_of < near_group, 2 * (NZ - dz), 2 * (NZ - dz) - 1)
    place = jnp.where(dz == 0, 0, jnp.where(dz == NZ // 2, NZ - 1, jnp.where(dz < NZ // 2, up, down)))
    offset = place * group + g_of
    offset_f = jnp.broadcast_to(offset.astype(F32), (rows, rows))
    same = offset_f == offset_f.T
    earlier = lax.broadcasted_iota(jnp.int32, (rows, rows), 0) < lax.broadcasted_iota(jnp.int32, (rows, rows), 1)
    rank = jnp.sum(jnp.where(same & earlier, 1.0, 0.0), axis=0, keepdims=True).astype(jnp.int32)
    target = offset * (2 * CAP) + rank
    targets = jnp.concatenate([target, target + CAP], axis=1)
    raw[0, 0, 0] = ids

    slab = group * 2 * CAP

    def pack(m):
        hit = lax.broadcasted_iota(jnp.int32, (slab, 2 * rows), 0) + m * slab == targets
        part = jnp.dot(jnp.where(hit, 1.0, 0.0).astype(BF16), halves[...], preferred_element_type=F32)
        send[m * group : (m + 1) * group] = part.astype(BF16).reshape(group, 2 * CAP, half)
        if m == 0:
            keys[0, 0] = send[0]

    def ship(m):
        @pl.loop(1 if m == 0 else 0, group)
        def _(g):
            k = m * group + g
            push(send.at[k], keys.at[0, k], row_send_sem, row_recv_sem.at[m], ahead(m, g))

    pack(0)
    pl.semaphore_wait(barrier, group - 1 + NZ - 1 + NY - 1)

    @pl.loop(1, group)
    def _(g):
        pl.semaphore_signal(ready_sem, inc=1, device_id=plane(g), device_id_type=MESH)

    ship(0)
    for m in range(1, min(AHEAD, NZ)):
        pack(m)
    pl.semaphore_wait(ready_sem, group - 1)
    for m in range(1, min(AHEAD, NZ)):
        ship(m)

    @pl.loop(1, NZ)
    def _(m):
        push(raw.at[0, 0, 0], raw.at[0, m, 0], raw_send_sem.at[0], raw_z_sem, ahead(m, 0))

    def raw_plane():
        wait_bytes(raw.at[0, pl.ds(1, NZ - 1), 0], raw_z_sem)

        @pl.loop(1, group)
        def _(g):
            push(raw.at[0, :, 0], raw.at[0, :, g], raw_send_sem.at[1], raw_plane_sem, plane(g))

    def raw_y():
        wait_bytes(raw.at[0, :, pl.ds(1, group - 1)], raw_plane_sem)
        for n, (to, column) in enumerate(((y_right, 1), (y_left, 3), (y_far, 2))):
            push(raw.at[0], raw.at[column], raw_send_sem.at[2 + n], raw_y_sem.at[n], (me, to))

    def read_ids(column):
        parts = []
        for m in range(NZ):
            parts += [raw[column, m, :near_group], raw[column, swap(m), near_group:]]
        ids_of = jnp.broadcast_to(jnp.concatenate(parts, axis=0), (owners, CAP, rows)).reshape(slots, rows)
        mine = lax.div(ids_of, per_owner) == me
        below = (
            lax.broadcasted_iota(jnp.int32, (rows, rows), 0) < lax.broadcasted_iota(jnp.int32, (rows, rows), 1)
        )
        ranks = jnp.dot(
            jnp.where(mine, 1.0, 0.0).astype(BF16), jnp.where(below, 1.0, 0.0).astype(BF16),
            preferred_element_type=F32,
        )
        slot_rank = lax.rem(lax.broadcasted_iota(jnp.int32, (slots, rows), 0), CAP).astype(F32)
        value = (lax.rem(ids_of, per_owner) + 1).astype(F32)
        chosen = jnp.where(mine & (ranks == slot_rank), value, 0.0).astype(BF16)
        key_ids[column] = lax.dot_general(
            jnp.ones((8, rows), BF16), chosen, (((1,), (1,)), ((), ())), preferred_element_type=F32
        ) - 1.0
        return chosen

    strip = min(128, owners * 2 * CAP)
    targets_f = jnp.broadcast_to(targets.astype(F32), (strip, 2 * rows)).T
    lanes = lax.broadcasted_iota(jnp.int32, (2 * rows, strip), 1).astype(F32)
    for j in range(owners * 2 * CAP // strip):
        turned[:, j * strip : (j + 1) * strip] = jnp.where(lanes + j * strip == targets_f, 1.0, 0.0).astype(BF16)

    def unpack(column, m):
        part = keys[column, m * group : (m + 1) * group].astype(F32)
        first = column * slots + m * chunk_rows
        table[first : first + chunk_rows, :half] = part[:, :CAP, :].reshape(chunk_rows, half).astype(BF16)
        table[first : first + chunk_rows, half:] = part[:, CAP:, :].reshape(chunk_rows, half).astype(BF16)

    def chunk(column, m):
        return keys.at[column, pl.ds(m * group, group)]

    def part_of(column, m, part):
        return keys.at[column, pl.ds(m * group + part * near_group, near_group)]

    def relay(m):
        for way, to, column in ((0, y_right, 1), (1, y_left, 3)):
            wait_bytes(chunk(column, m), y_recv_sem.at[way, m])
            push(part_of(column, m, way), part_of(2, m, way), relay_send_sem.at[way], far_recv_sem.at[way, m], (me, to))
        unpack(1, m)
        unpack(3, m)

    for m in range(NZ):
        if m + AHEAD < NZ:
            pack(m + AHEAD)
            ship(m + AHEAD)
        arriving = keys.at[0, pl.ds(1, group - 1)] if m == 0 else chunk(0, m)
        wait_bytes(arriving, row_recv_sem.at[m])
        push(chunk(0, m), chunk(1, m), y_send_sem.at[0], y_recv_sem.at[0, m], (me, y_right))
        push(chunk(0, m), chunk(3, m), y_send_sem.at[1], y_recv_sem.at[1, m], (me, y_left))
        unpack(0, m)
        if m == min(1, NZ - 1):
            raw_plane()
        if m >= 1:
            relay(m - 1)
        if m == min(3, NZ - 1):
            raw_y()
        if m >= 2:
            for way in range(2):
                wait_bytes(part_of(2, m - 2, way), far_recv_sem.at[way, m - 2])
            unpack(2, m - 2)
    relay(NZ - 1)

    chosen = read_ids(0)
    query_id = jnp.dot(chosen, jnp.ones((rows, 128), BF16), preferred_element_type=F32)[:, 0:1] - 1.0
    query_temp = jnp.ones_like(query_id)
    for c in range(per_owner):
        query_temp = jnp.where(query_id == float(c), temp_ref[c], query_temp)
    query_id = jnp.where(query_id < 0.0, -2.0, query_id)
    for n, column in enumerate((1, 3, 2)):
        wait_bytes(raw.at[column], raw_y_sem.at[n])
        read_ids(column)

    block = min(256, slots)
    best = [jnp.full((block, 1), LOWEST, F32) for _ in range(slots // block)]
    for column in (0, 1, 3, 2):
        if column == 2:
            for m in range(max(NZ - 2, 0), NZ):
                for way in range(2):
                    wait_bytes(part_of(2, m, way), far_recv_sem.at[way, m])
                unpack(2, m)
        for b in range(slots // block - 1, -1, -1):
            cosine = lax.dot_general(
                table[b * block : (b + 1) * block, :],
                table[column * slots : (column + 1) * slots, :],
                (((1,), (1,)), ((), ())),
                preferred_element_type=F32,
            )
            allowed = query_id[b * block : (b + 1) * block] == key_ids[column, 0:1, :]
            if column == 0:
                allowed &= (
                    lax.broadcasted_iota(jnp.int32, (block, slots), 0) + b * block
                    != lax.broadcasted_iota(jnp.int32, (block, slots), 1)
                )
            score = jnp.where(allowed, cosine * query_temp[b * block : (b + 1) * block], LOWEST)
            scores[b * block : (b + 1) * block, column * slots : (column + 1) * slots] = score
            best[b] = jnp.maximum(best[b], jnp.max(score, axis=1, keepdims=True))

    per_block = block // CAP
    for b in range(slots // block):
        close = best[b] / query_temp[b * block : (b + 1) * block]
        lane = lax.broadcasted_iota(jnp.int32, (block, 128), 1)
        rank_of = lax.rem(lax.broadcasted_iota(jnp.int32, (block, 128), 0), CAP)
        spread_close = jnp.sum(jnp.where(lane == rank_of, close, 0.0).reshape(per_block, CAP, 128), axis=1)
        for j in range(per_block):
            m, g = divmod(b * per_block + j, group)
            sim_send[m if g < near_group else swap(m), g] = spread_close[j : j + 1, :]
    sim_mid[0] = sim_send[0]

    @pl.loop(1, NZ)
    def _(m):
        push(sim_send.at[m], sim_mid.at[m], sim_send_sem.at[0], sim_z_sem, behind(m, 0))

    for b in range(slots // block - 1, -1, -1):
        here = pl.ds(b * block, block)
        total = jnp.zeros((block, 1), F32)
        for column in range(NY):
            weight = jnp.exp(scores[here, column * slots : (column + 1) * slots] - best[b])
            total += jnp.sum(weight, axis=1, keepdims=True)
            weights[:, column * slots : (column + 1) * slots] = weight.astype(BF16)
        near = []
        for h in range(2):
            summed = jnp.dot(weights[...], table[:, h * half : (h + 1) * half], preferred_element_type=F32)
            near.append((summed / total).reshape(per_block, CAP, half))
        outs[pl.ds(b * per_block, per_block)] = jnp.concatenate(near, axis=1).astype(BF16)
        if b == 0:
            back[0] = outs[0]

        for m in range((b + 1) * per_block // group - 1, b * per_block // group - 1, -1):
            @pl.loop(1 if m == 0 else 0, group)
            def _(g):
                k = m * group + g
                push(outs.at[k], back.at[k], back_send_sem, back_recv_sem, behind(m, g))

        if b == slots // block - 1:
            wait_bytes(sim_mid.at[pl.ds(1, NZ - 1)], sim_z_sem)
            sim_recv[:, 0] = sim_mid[:, 0]

            @pl.loop(1, group)
            def _(g):
                push(sim_mid.at[:, g], sim_recv.at[:, g], sim_send_sem.at[1], sim_plane_sem, plane_back(g))

    others = pl.ds(1, owners - 1)
    wait_bytes(sim_recv.at[:, pl.ds(1, group - 1)], sim_plane_sem)
    got = []
    for k in range(owners):
        m, g = divmod(k, group)
        got.append(sim_recv[m if g < near_group else swap(m), g])
    at_offset = lax.broadcasted_iota(jnp.int32, (owners, rows), 0) == offset
    at_rank = lax.broadcasted_iota(jnp.int32, (128, rows), 0) == rank
    picked = lax.dot_general(
        jnp.concatenate(got, axis=0), jnp.where(at_offset, 1.0, 0.0), (((0,), (0,)), ((), ())),
        preferred_element_type=F32, precision=lax.Precision.HIGHEST,
    )
    sim_ref[...] = jnp.sum(jnp.where(at_rank, picked, 0.0), axis=0, keepdims=True)

    wait_bytes(send.at[others], row_send_sem)
    wait_bytes(sim_send.at[pl.ds(1, NZ - 1)], sim_send_sem.at[0])
    wait_bytes(sim_mid.at[:, pl.ds(1, group - 1)], sim_send_sem.at[1])
    wait_bytes(raw.at[0, pl.ds(1, NZ - 1), 0], raw_send_sem.at[0])
    wait_bytes(raw.at[0, :, pl.ds(1, group - 1)], raw_send_sem.at[1])
    for n in range(3):
        wait_bytes(raw.at[0], raw_send_sem.at[2 + n])
    for way in range(2):
        wait_bytes(keys.at[0], y_send_sem.at[way])
        wait_bytes(keys.at[0, pl.ds(0, owners // 2)], relay_send_sem.at[way])

    wait_bytes(back.at[others], back_recv_sem)
    returned = jnp.dot(
        turned[...], back[...].reshape(owners * 2 * CAP, half), preferred_element_type=F32
    )
    out_ref[:, :half] = unit[:, :half] - returned[:rows]
    out_ref[:, half:] = unit[:, half:] - returned[rows:]
    wait_bytes(outs.at[others], back_send_sem)


def per_device(embeds, cluster_ids, inv_temp):
    rows, width = embeds.shape
    group = NX * NC
    owners = group * NZ
    slots = owners * CAP
    half = width // 2
    block = min(256, slots)
    DMA = pltpu.SemaphoreType.DMA
    vmem = pl.BlockSpec(memory_space=pltpu.VMEM)
    hbm = pl.BlockSpec(memory_space=pltpu.HBM)
    residual, similarity = pl.pallas_call(
        kernel,
        out_shape=(jax.ShapeDtypeStruct((rows, width), F32), jax.ShapeDtypeStruct((1, rows), F32)),
        in_specs=[hbm, hbm, pl.BlockSpec(memory_space=pltpu.SMEM)],
        out_specs=(vmem, vmem),
        scratch_shapes=[
            pltpu.VMEM((1, rows), jnp.int32),
            pltpu.VMEM((rows, width), F32),
            pltpu.VMEM((rows, width), F32),
            pltpu.VMEM((2 * rows, half), BF16),
            pltpu.VMEM((owners, 2 * CAP, half), BF16),
            pltpu.VMEM((NY, owners, 2 * CAP, half), BF16),
            pltpu.VMEM((NY * slots, width), BF16),
            pltpu.VMEM((slots, NY * slots), F32),
            pltpu.VMEM((block, NY * slots), BF16),
            pltpu.VMEM((owners, 2 * CAP, half), BF16),
            pltpu.VMEM((owners, 2 * CAP, half), BF16),
            pltpu.VMEM((2 * rows, owners * 2 * CAP), BF16),
            pltpu.VMEM((NY, NZ, group, 1, rows), jnp.int32),
            pltpu.VMEM((NY, 8, slots), F32),
            pltpu.VMEM((NZ, group, 1, 128), F32),
            pltpu.VMEM((NZ, group, 1, 128), F32),
            pltpu.VMEM((NZ, group, 1, 128), F32),
            DMA((2,)), pltpu.SemaphoreType.REGULAR, DMA, DMA((NZ,)), DMA((2,)), DMA((2,)),
            DMA((2, NZ)), DMA((2, NZ)), DMA((5,)), DMA, DMA, DMA((3,)),
            DMA, DMA, DMA((2,)), DMA, DMA,
        ],
        compiler_params=pltpu.CompilerParams(
            collective_id=0, has_side_effects=True, vmem_limit_bytes=48 * 1024 * 1024
        ),
    )(cluster_ids.reshape(1, rows), embeds, inv_temp)
    return residual, similarity.reshape(rows)


def solution(mesh):
    in_specs = (P(("dp", "clus"), None), P(("dp", "clus")), P("dp"))
    out_specs = (P(("dp", "clus"), None), P(("dp", "clus")))
    return jax.shard_map(
        per_device, mesh=mesh, in_specs=in_specs, out_specs=out_specs, check_vma=False
    )
```

time: 108 us -> 85.8 us (0.79)
  Pallas kernels: 104 us -> 82 us
    pallas_call x1, Pallas kernels: 104 us -> 82 us  [per_device(): pl.pallas_call(kernel, out_shape=(jax.ShapeDtypeStruct((rows, width), F32...]
where the time goes in v2:
time: 85.8 us; the launch traced here: 85.6 us
  Pallas kernels  82 us (96%)
  local copies, waits for them, and re-layouts  3 us (3%)
    pallas_call x1, Pallas kernels, per_device(): pl.pallas_call(kernel, out_shape=(jax.ShapeDtypeStruct((rows, width), F32...  82 us
    unnamed x8, local copies, waits for them, and re-layouts  3 us

profile of v2, /device:TPU:1, one launch (start us, length us, event | category | flops | bytes accessed | tf_op | source)
XLA Modules:
  0.0 85.6 jit_solution(2252225610518860493)
XLA Ops:
  0.6 0.0 copy-start.2
  0.6 0.0 copy-start.1
  0.6 0.6 copy-done.2
  1.3 0.0 copy-done.1
  1.3 0.0 copy-start
  1.3 1.0 %copy-done = f32[128,1024]{1,0:T(8,128)S(1)} copy-done((f32[128,1024]{1,0:T(8,128)S(1)}, f32[128,1024]{1,0:T(8,128)}, u32[]{:S(2)}) %copy-start) | copy-done | bytes 524312
  2.3 82.0 %shard_map.50 = (f32[128,1024]{1,0:T(8,128)S(1)}, f32[1,128]{1,0:T(1,128)S(1)}) custom-call(s32[1,128]{1,0:T(1,128)S(1)} %bitcast.2, f32[128,1024]{1,0:T(8,128)S(1)} %copy-done, f32[4]{0:T(128)S(1)} %copy-done.2), custom_call_target="tpu_custom_call" | custom-call | tf_op jit(solution)/shard_map/pallas_call | solution.py:364
  84.3 0.8 copy.7
  85.1 0.5 copy.8
Async XLA Ops:
  0.6 0.7 copy-start.2
  0.6 0.7 copy-start.1
  1.3 1.0 %copy-start = (f32[128,1024]{1,0:T(8,128)S(1)}, f32[128,1024]{1,0:T(8,128)}, u32[]{:S(2)}) copy-start(f32[128,1024]{1,0:T(8,128)} %x_hbm.1) | copy-start | bytes 1572868

commit v3 on v2

--- a/solution.py
+++ b/solution.py
@@ -10,7 +10,7 @@
 NX, NZ, NC, NY = 4, 8, 2, 4
 CAP = 8
 LOWEST = -1e30
-AHEAD = 4
+AHEAD = 2
 MESH = pl.DeviceIdType.MESH
 F32 = jnp.float32
 BF16 = jnp.bfloat16
@@ -21,8 +21,8 @@
 
 
 def kernel(
-    ids_hbm, x_hbm, temp_ref, out_ref, sim_ref,
-    ids_ref, x_ref, unit, halves, send, keys, table, scores, weights, outs, back, turned,
+    ids_hbm, x_hbm, temp_hbm, out_ref, sim_ref,
+    ids_ref, x_ref, temp_ref, unit, halves, send, keys, table, scores, weights, outs, back, turned,
     raw, key_ids, sim_send, sim_mid, sim_recv,
     load_sem, ready_sem, row_send_sem, row_recv_sem, y_send_sem, relay_send_sem,
     y_recv_sem, far_recv_sem, raw_send_sem, raw_z_sem, raw_plane_sem, raw_y_sem,
@@ -82,6 +82,7 @@
     loads = [
         pltpu.make_async_copy(x_hbm, x_ref, load_sem.at[0]),
         pltpu.make_async_copy(ids_hbm, ids_ref, load_sem.at[1]),
+        pltpu.make_async_copy(temp_hbm, temp_ref, load_sem.at[2]),
     ]
     for load in loads:
         load.start()
@@ -99,8 +100,8 @@
     for y in (y_right, y_left, y_far):
         pl.semaphore_signal(barrier, inc=1, device_id=(me, y), device_id_type=MESH)
 
-    loads[1].wait()
-    loads[0].wait()
+    for load in loads:
+        load.wait()
     x = x_ref[...]
     unit_rows = x * lax.rsqrt(jnp.sum(x * x, axis=1, keepdims=True) + 1e-06)
     unit[...] = unit_rows
@@ -139,7 +140,7 @@
         @pl.loop(1 if m == 0 else 0, group)
         def _(g):
             k = m * group + g
-            push(send.at[k], keys.at[0, k], row_send_sem, row_recv_sem.at[m], ahead(m, g))
+            push(send.at[k], keys.at[0, k], row_send_sem, row_recv_sem.at[lax.div(g, near_group), m], ahead(m, g))
 
     pack(0)
     pl.semaphore_wait(barrier, group - 1 + NZ - 1 + NY - 1)
@@ -217,14 +218,58 @@
         unpack(1, m)
         unpack(3, m)
 
+    block = min(256, slots)
+    blocks = slots // block
+    best = [jnp.full((block, 1), LOWEST, F32) for _ in range(blocks)]
+    query = []
+
+    def read_all_ids():
+        chosen = read_ids(0)
+        query_id = jnp.dot(chosen, jnp.ones((rows, 128), BF16), preferred_element_type=F32)[:, 0:1] - 1.0
+        query_temp = jnp.ones_like(query_id)
+        for c in range(per_owner):
+            query_temp = jnp.where(query_id == float(c), temp_ref[c], query_temp)
+        query.append(jnp.where(query_id < 0.0, -2.0, query_id))
+        query.append(query_temp)
+        for n, column in enumerate((1, 3, 2)):
+            wait_bytes(raw.at[column], raw_y_sem.at[n])
+            read_ids(column)
+
+    def score(column, first, count):
+        query_id, query_temp = query
+        base = column * slots + first
+        for b in range(blocks - 1, -1, -1):
+            at = slice(b * block, (b + 1) * block)
+            cosine = lax.dot_general(
+                table[at, :], table[base : base + count, :], (((1,), (1,)), ((), ())),
+                preferred_element_type=F32,
+            )
+            allowed = query_id[at] == key_ids[column, 0:1, first : first + count]
+            if column == 0:
+                allowed &= (
+                    lax.broadcasted_iota(jnp.int32, (block, count), 0) + b * block
+                    != lax.broadcasted_iota(jnp.int32, (block, count), 1) + first
+                )
+            scored = jnp.where(allowed, cosine * query_temp[at], LOWEST)
+            scores[at, base : base + count] = scored
+            best[b] = jnp.maximum(best[b], jnp.max(scored, axis=1, keepdims=True))
+
+    def far(m):
+        for way in range(2):
+            wait_bytes(part_of(2, m, way), far_recv_sem.at[way, m])
+        unpack(2, m)
+
     for m in range(NZ):
         if m + AHEAD < NZ:
             pack(m + AHEAD)
             ship(m + AHEAD)
-        arriving = keys.at[0, pl.ds(1, group - 1)] if m == 0 else chunk(0, m)
-        wait_bytes(arriving, row_recv_sem.at[m])
-        push(chunk(0, m), chunk(1, m), y_send_sem.at[0], y_recv_sem.at[0, m], (me, y_right))
-        push(chunk(0, m), chunk(3, m), y_send_sem.at[1], y_recv_sem.at[1, m], (me, y_left))
+        for part in range(2):
+            first = m * group + part * near_group
+            mine = 1 if first == 0 else 0
+            if near_group > mine:
+                wait_bytes(keys.at[0, pl.ds(first + mine, near_group - mine)], row_recv_sem.at[part, m])
+            push(part_of(0, m, part), part_of(1, m, part), y_send_sem.at[0], y_recv_sem.at[0, m], (me, y_right))
+            push(part_of(0, m, part), part_of(3, m, part), y_send_sem.at[1], y_recv_sem.at[1, m], (me, y_left))
         unpack(0, m)
         if m == min(1, NZ - 1):
             raw_plane()
@@ -233,62 +278,54 @@
         if m == min(3, NZ - 1):
             raw_y()
         if m >= 2:
-            for way in range(2):
-                wait_bytes(part_of(2, m - 2, way), far_recv_sem.at[way, m - 2])
-            unpack(2, m - 2)
+            far(m - 2)
+        if m == min(5, NZ - 1):
+            read_all_ids()
+        if m == NZ - 1:
+            score(0, 0, slots)
     relay(NZ - 1)
-
-    chosen = read_ids(0)
-    query_id = jnp.dot(chosen, jnp.ones((rows, 128), BF16), preferred_element_type=F32)[:, 0:1] - 1.0
-    query_temp = jnp.ones_like(query_id)
-    for c in range(per_owner):
-        query_temp = jnp.where(query_id == float(c), temp_ref[c], query_temp)
-    query_id = jnp.where(query_id < 0.0, -2.0, query_id)
-    for n, column in enumerate((1, 3, 2)):
-        wait_bytes(raw.at[column], raw_y_sem.at[n])
-        read_ids(column)
-
-    block = min(256, slots)
-    best = [jnp.full((block, 1), LOWEST, F32) for _ in range(slots // block)]
-    for column in (0, 1, 3, 2):
-        if column == 2:
-            for m in range(max(NZ - 2, 0), NZ):
-                for way in range(2):
-                    wait_bytes(part_of(2, m, way), far_recv_sem.at[way, m])
-                unpack(2, m)
-        for b in range(slots // block - 1, -1, -1):
-            cosine = lax.dot_general(
-                table[b * block : (b + 1) * block, :],
-                table[column * slots : (column + 1) * slots, :],
-                (((1,), (1,)), ((), ())),
-                preferred_element_type=F32,
-            )
-            allowed = query_id[b * block : (b + 1) * block] == key_ids[column, 0:1, :]
-            if column == 0:
-                allowed &= (
-                    lax.broadcasted_iota(jnp.int32, (block, slots), 0) + b * block
-                    != lax.broadcasted_iota(jnp.int32, (block, slots), 1)
-                )
-            score = jnp.where(allowed, cosine * query_temp[b * block : (b + 1) * block], LOWEST)
-            scores[b * block : (b + 1) * block, column * slots : (column + 1) * slots] = score
-            best[b] = jnp.maximum(best[b], jnp.max(score, axis=1, keepdims=True))
+    score(1, 0, slots)
+    score(3, 0, slots)
+    half_slots = slots // 2
+    late = range(max(NZ - 2, 0), NZ)
+    for m in late:
+        if m < NZ // 2:
+            far(m)
+    score(2, 0, half_slots)
+    for m in late:
+        if m >= NZ // 2:
+            far(m)
+    score(2, half_slots, half_slots)
+    query_temp = query[1]
 
     per_block = block // CAP
-    for b in range(slots // block):
-        close = best[b] / query_temp[b * block : (b + 1) * block]
-        lane = lax.broadcasted_iota(jnp.int32, (block, 128), 1)
-        rank_of = lax.rem(lax.broadcasted_iota(jnp.int32, (block, 128), 0), CAP)
-        spread_close = jnp.sum(jnp.where(lane == rank_of, close, 0.0).reshape(per_block, CAP, 128), axis=1)
-        for j in range(per_block):
-            m, g = divmod(b * per_block + j, group)
-            sim_send[m if g < near_group else swap(m), g] = spread_close[j : j + 1, :]
-    sim_mid[0] = sim_send[0]
-
-    @pl.loop(1, NZ)
-    def _(m):
-        push(sim_send.at[m], sim_mid.at[m], sim_send_sem.at[0], sim_z_sem, behind(m, 0))
-
-    for b in range(slots // block - 1, -1, -1):
+
+    def similarities():
+        for b in range(slots // block):
+            close = best[b] / query_temp[b * block : (b + 1) * block]
+            lane = lax.broadcasted_iota(jnp.int32, (block, 128), 1)
+            rank_of = lax.rem(lax.broadcasted_iota(jnp.int32, (block, 128), 0), CAP)
+            spread_close = jnp.sum(jnp.where(lane == rank_of, close, 0.0).reshape(per_block, CAP, 128), axis=1)
+            for j in range(per_block):
+                m, g = divmod(b * per_block + j, group)
+                sim_send[m if g < near_group else swap(m), g] = spread_close[j : j + 1, :]
+        sim_mid[0] = sim_send[0]
+
+        @pl.loop(1, NZ)
+        def _(m):
+            push(sim_send.at[m], sim_mid.at[m], sim_send_sem.at[0], sim_z_sem, behind(m, 0))
+
+
+    def way_back(m):
+        @pl.loop(1 if m == 0 else 0, group)
+        def _(g):
+            k = m * group + g
+            push(outs.at[k], back.at[k], back_send_sem, back_recv_sem.at[back_part(m)], behind(m, g))
+
+    def back_part(m):
+        return m * chunk_rows // block
+
+    for b in range(blocks - 1, -1, -1):
         here = pl.ds(b * block, block)
         total = jnp.zeros((block, 1), F32)
         for column in range(NY):
@@ -302,20 +339,21 @@
         outs[pl.ds(b * per_block, per_block)] = jnp.concatenate(near, axis=1).astype(BF16)
         if b == 0:
             back[0] = outs[0]
-
-        for m in range((b + 1) * per_block // group - 1, b * per_block // group - 1, -1):
-            @pl.loop(1 if m == 0 else 0, group)
-            def _(g):
-                k = m * group + g
-                push(outs.at[k], back.at[k], back_send_sem, back_recv_sem, behind(m, g))
-
-        if b == slots // block - 1:
+        if b == blocks - 2 or blocks == 1:
+            if blocks == 1:
+                similarities()
             wait_bytes(sim_mid.at[pl.ds(1, NZ - 1)], sim_z_sem)
             sim_recv[:, 0] = sim_mid[:, 0]
 
             @pl.loop(1, group)
             def _(g):
                 push(sim_mid.at[:, g], sim_recv.at[:, g], sim_send_sem.at[1], sim_plane_sem, plane_back(g))
+
+        chunks = list(range((b + 1) * per_block // group - 1, b * per_block // group - 1, -1))
+        for n, m in enumerate(chunks):
+            way_back(m)
+            if n == 1 and b == blocks - 1 and blocks > 1:
+                similarities()
 
     others = pl.ds(1, owners - 1)
     wait_bytes(sim_recv.at[:, pl.ds(1, group - 1)], sim_plane_sem)
@@ -342,12 +380,21 @@
         wait_bytes(keys.at[0], y_send_sem.at[way])
         wait_bytes(keys.at[0, pl.ds(0, owners // 2)], relay_send_sem.at[way])
 
-    wait_bytes(back.at[others], back_recv_sem)
-    returned = jnp.dot(
-        turned[...], back[...].reshape(owners * 2 * CAP, half), preferred_element_type=F32
-    )
-    out_ref[:, :half] = unit[:, :half] - returned[:rows]
-    out_ref[:, half:] = unit[:, half:] - returned[rows:]
+    span = 2 * block
+    for b in range(blocks - 1, -1, -1):
+        first = max(b * per_block, 1)
+        wait_bytes(back.at[pl.ds(first, (b + 1) * per_block - first)], back_recv_sem.at[b])
+        returned = jnp.dot(
+            turned[:, b * span : (b + 1) * span],
+            back[b * per_block : (b + 1) * per_block].reshape(span, half),
+            preferred_element_type=F32,
+        )
+        if b > 0:
+            unit[:, :half] -= returned[:rows]
+            unit[:, half:] -= returned[rows:]
+        else:
+            out_ref[:, :half] = unit[:, :half] - returned[:rows]
+            out_ref[:, half:] = unit[:, half:] - returned[rows:]
     wait_bytes(outs.at[others], back_send_sem)
 
 
@@ -364,11 +411,12 @@
     residual, similarity = pl.pallas_call(
         kernel,
         out_shape=(jax.ShapeDtypeStruct((rows, width), F32), jax.ShapeDtypeStruct((1, rows), F32)),
-        in_specs=[hbm, hbm, pl.BlockSpec(memory_space=pltpu.SMEM)],
+        in_specs=[hbm, hbm, hbm],
         out_specs=(vmem, vmem),
         scratch_shapes=[
             pltpu.VMEM((1, rows), jnp.int32),
             pltpu.VMEM((rows, width), F32),
+            pltpu.SMEM(inv_temp.shape, F32),
             pltpu.VMEM((rows, width), F32),
             pltpu.VMEM((2 * rows, half), BF16),
             pltpu.VMEM((owners, 2 * CAP, half), BF16),
@@ -384,14 +432,14 @@
             pltpu.VMEM((NZ, group, 1, 128), F32),
             pltpu.VMEM((NZ, group, 1, 128), F32),
             pltpu.VMEM((NZ, group, 1, 128), F32),
-            DMA((2,)), pltpu.SemaphoreType.REGULAR, DMA, DMA((NZ,)), DMA((2,)), DMA((2,)),
+            DMA((3,)), pltpu.SemaphoreType.REGULAR, DMA, DMA((2, NZ)), DMA((2,)), DMA((2,)),
             DMA((2, NZ)), DMA((2, NZ)), DMA((5,)), DMA, DMA, DMA((3,)),
-            DMA, DMA, DMA((2,)), DMA, DMA,
+            DMA, DMA((2,)), DMA((2,)), DMA, DMA,
         ],
         compiler_params=pltpu.CompilerParams(
             collective_id=0, has_side_effects=True, vmem_limit_bytes=48 * 1024 * 1024
         ),
-    )(cluster_ids.reshape(1, rows), embeds, inv_temp)
+    )(*(pltpu.with_memory_space_constraint(a, pltpu.HBM) for a in (cluster_ids.reshape(1, rows), embeds, inv_temp)))
     return residual, similarity.reshape(rows)
 
 

time: 85.8 us -> 82.3 us (0.959)
  Pallas kernels: 82 us -> 80.3 us
  local copies, waits for them, and re-layouts: 3 us -> 1.31 us
    pallas_call x1, Pallas kernels: 82 us -> 80.3 us  [per_device(): pl.pallas_call(kernel, out_shape=(jax.ShapeDtypeStruct((rows, width), F32...]
    unnamed x8 -> x2, local copies, waits for them, and re-layouts: 3 us -> 1.31 us
where the time goes in v3:
time: 82.3 us; the launch traced here: 82.2 us
  Pallas kernels  80.3 us (98%)
  local copies, waits for them, and re-layouts  1.31 us (2%)
    pallas_call x1, Pallas kernels, per_device(): pl.pallas_call(kernel, out_shape=(jax.ShapeDtypeStruct((rows, width), F32...  80.3 us

profile of v3, /device:TPU:1, one launch (start us, length us, event | category | flops | bytes accessed | tf_op | source)
XLA Modules:
  0.0 82.2 jit_solution(4264315691928922535)
XLA Ops:
  0.6 80.3 %shard_map.50 = (f32[128,1024]{1,0:T(8,128)S(1)}, f32[1,128]{1,0:T(1,128)S(1)}) custom-call(s32[1,128]{1,0:T(1,128)} %bitcast.3, f32[128,1024]{1,0:T(8,128)} %x_hbm.1, f32[4]{0:T(128)} %temp_hbm.1), custom_call_target="tpu_custom_call" | custom-call | tf_op jit(solution)/shard_map/pallas_call | solution.py:411
  80.9 0.8 copy.7
  81.7 0.5 copy.8

commit v4 on v3

--- a/solution.py
+++ b/solution.py
@@ -10,7 +10,8 @@
 NX, NZ, NC, NY = 4, 8, 2, 4
 CAP = 8
 LOWEST = -1e30
-AHEAD = 2
+FINE = 128
+AHEAD = 3
 MESH = pl.DeviceIdType.MESH
 F32 = jnp.float32
 BF16 = jnp.bfloat16
@@ -220,6 +221,7 @@
 
     block = min(256, slots)
     blocks = slots // block
+    every = range(blocks - 1, -1, -1)
     best = [jnp.full((block, 1), LOWEST, F32) for _ in range(blocks)]
     query = []
 
@@ -235,10 +237,10 @@
             wait_bytes(raw.at[column], raw_y_sem.at[n])
             read_ids(column)
 
-    def score(column, first, count):
+    def score(column, first, count, which):
         query_id, query_temp = query
         base = column * slots + first
-        for b in range(blocks - 1, -1, -1):
+        for b in which:
             at = slice(b * block, (b + 1) * block)
             cosine = lax.dot_general(
                 table[at, :], table[base : base + count, :], (((1,), (1,)), ((), ())),
@@ -260,9 +262,6 @@
         unpack(2, m)
 
     for m in range(NZ):
-        if m + AHEAD < NZ:
-            pack(m + AHEAD)
-            ship(m + AHEAD)
         for part in range(2):
             first = m * group + part * near_group
             mine = 1 if first == 0 else 0
@@ -270,6 +269,9 @@
                 wait_bytes(keys.at[0, pl.ds(first + mine, near_group - mine)], row_recv_sem.at[part, m])
             push(part_of(0, m, part), part_of(1, m, part), y_send_sem.at[0], y_recv_sem.at[0, m], (me, y_right))
             push(part_of(0, m, part), part_of(3, m, part), y_send_sem.at[1], y_recv_sem.at[1, m], (me, y_left))
+        if m + AHEAD < NZ:
+            pack(m + AHEAD)
+            ship(m + AHEAD)
         unpack(0, m)
         if m == min(1, NZ - 1):
             raw_plane()
@@ -282,20 +284,20 @@
         if m == min(5, NZ - 1):
             read_all_ids()
         if m == NZ - 1:
-            score(0, 0, slots)
+            score(0, 0, slots, every)
     relay(NZ - 1)
-    score(1, 0, slots)
-    score(3, 0, slots)
+    score(1, 0, slots, every)
+    score(3, 0, slots, every)
     half_slots = slots // 2
     late = range(max(NZ - 2, 0), NZ)
     for m in late:
         if m < NZ // 2:
             far(m)
-    score(2, 0, half_slots)
+    score(2, 0, half_slots, every)
     for m in late:
         if m >= NZ // 2:
             far(m)
-    score(2, half_slots, half_slots)
+    score(2, half_slots, half_slots, [blocks - 1])
     query_temp = query[1]
 
     per_block = block // CAP
@@ -323,25 +325,30 @@
             push(outs.at[k], back.at[k], back_send_sem, back_recv_sem.at[back_part(m)], behind(m, g))
 
     def back_part(m):
-        return m * chunk_rows // block
-
-    for b in range(blocks - 1, -1, -1):
-        here = pl.ds(b * block, block)
-        total = jnp.zeros((block, 1), F32)
+        return m * chunk_rows // fine
+
+    fine = min(FINE, block)
+    per_fine = fine // CAP
+    parts = slots // fine
+    for p in range(parts - 1, -1, -1):
+        b, inner = divmod(p * fine, block)
+        here = pl.ds(p * fine, fine)
+        top = best[b][inner : inner + fine]
+        total = jnp.zeros((fine, 1), F32)
         for column in range(NY):
-            weight = jnp.exp(scores[here, column * slots : (column + 1) * slots] - best[b])
+            weight = jnp.exp(scores[here, column * slots : (column + 1) * slots] - top)
             total += jnp.sum(weight, axis=1, keepdims=True)
-            weights[:, column * slots : (column + 1) * slots] = weight.astype(BF16)
+            weights[:fine, column * slots : (column + 1) * slots] = weight.astype(BF16)
         near = []
         for h in range(2):
-            summed = jnp.dot(weights[...], table[:, h * half : (h + 1) * half], preferred_element_type=F32)
-            near.append((summed / total).reshape(per_block, CAP, half))
-        outs[pl.ds(b * per_block, per_block)] = jnp.concatenate(near, axis=1).astype(BF16)
-        if b == 0:
+            summed = jnp.dot(weights[:fine], table[:, h * half : (h + 1) * half], preferred_element_type=F32)
+            near.append((summed / total).reshape(per_fine, CAP, half))
+        outs[pl.ds(p * per_fine, per_fine)] = jnp.concatenate(near, axis=1).astype(BF16)
+        if p == 0:
             back[0] = outs[0]
-        if b == blocks - 2 or blocks == 1:
-            if blocks == 1:
-                similarities()
+        if parts == 1:
+            similarities()
+        if p == max(parts // 2 - 1, 0):
             wait_bytes(sim_mid.at[pl.ds(1, NZ - 1)], sim_z_sem)
             sim_recv[:, 0] = sim_mid[:, 0]
 
@@ -349,10 +356,10 @@
             def _(g):
                 push(sim_mid.at[:, g], sim_recv.at[:, g], sim_send_sem.at[1], sim_plane_sem, plane_back(g))
 
-        chunks = list(range((b + 1) * per_block // group - 1, b * per_block // group - 1, -1))
-        for n, m in enumerate(chunks):
+        for n, m in enumerate(range((p + 1) * per_fine // group - 1, p * per_fine // group - 1, -1)):
             way_back(m)
-            if n == 1 and b == blocks - 1 and blocks > 1:
+            if p == parts - 1 and parts > 1 and n == 1:
+                score(2, half_slots, half_slots, range(blocks - 2, -1, -1))
                 similarities()
 
     others = pl.ds(1, owners - 1)
@@ -380,16 +387,16 @@
         wait_bytes(keys.at[0], y_send_sem.at[way])
         wait_bytes(keys.at[0, pl.ds(0, owners // 2)], relay_send_sem.at[way])
 
-    span = 2 * block
-    for b in range(blocks - 1, -1, -1):
-        first = max(b * per_block, 1)
-        wait_bytes(back.at[pl.ds(first, (b + 1) * per_block - first)], back_recv_sem.at[b])
+    span = 2 * fine
+    for p in range(parts - 1, -1, -1):
+        first = max(p * per_fine, 1)
+        wait_bytes(back.at[pl.ds(first, (p + 1) * per_fine - first)], back_recv_sem.at[p])
         returned = jnp.dot(
-            turned[:, b * span : (b + 1) * span],
-            back[b * per_block : (b + 1) * per_block].reshape(span, half),
+            turned[:, p * span : (p + 1) * span],
+            back[p * per_fine : (p + 1) * per_fine].reshape(span, half),
             preferred_element_type=F32,
         )
-        if b > 0:
+        if p > 0:
             unit[:, :half] -= returned[:rows]
             unit[:, half:] -= returned[rows:]
         else:
@@ -434,7 +441,7 @@
             pltpu.VMEM((NZ, group, 1, 128), F32),
             DMA((3,)), pltpu.SemaphoreType.REGULAR, DMA, DMA((2, NZ)), DMA((2,)), DMA((2,)),
             DMA((2, NZ)), DMA((2, NZ)), DMA((5,)), DMA, DMA, DMA((3,)),
-            DMA, DMA((2,)), DMA((2,)), DMA, DMA,
+            DMA, DMA((slots // min(FINE, slots),)), DMA((2,)), DMA, DMA,
         ],
         compiler_params=pltpu.CompilerParams(
             collective_id=0, has_side_effects=True, vmem_limit_bytes=48 * 1024 * 1024

time: 82.3 us -> 81.3 us (0.988)
  Pallas kernels: 80.3 us -> 79.2 us
    pallas_call x1, Pallas kernels: 80.3 us -> 79.2 us  [per_device(): pl.pallas_call(kernel, out_shape=(jax.ShapeDtypeStruct((rows, width), F32...]
where the time goes in v4:
time: 81.3 us; the launch traced here: 81.2 us
  Pallas kernels  79.2 us (97%)
  local copies, waits for them, and re-layouts  1.31 us (2%)
    pallas_call x1, Pallas kernels, per_device(): pl.pallas_call(kernel, out_shape=(jax.ShapeDtypeStruct((rows, width), F32...  79.2 us

profile of v4, /device:TPU:1, one launch (start us, length us, event | category | flops | bytes accessed | tf_op | source)
XLA Modules:
  0.0 81.2 jit_solution(1616639193800161488)
XLA Ops:
  0.6 79.2 %shard_map.50 = (f32[128,1024]{1,0:T(8,128)S(1)}, f32[1,128]{1,0:T(1,128)S(1)}) custom-call(s32[1,128]{1,0:T(1,128)} %bitcast.3, f32[128,1024]{1,0:T(8,128)} %x_hbm.1, f32[4]{0:T(128)} %temp_hbm.1), custom_call_target="tpu_custom_call" | custom-call | tf_op jit(solution)/shard_map/pallas_call | solution.py:418
  79.9 0.8 copy.7
  80.7 0.5 copy.8

commit v5 on v4

--- a/solution.py
+++ b/solution.py
@@ -170,8 +170,9 @@
 
     def raw_y():
         wait_bytes(raw.at[0, :, pl.ds(1, group - 1)], raw_plane_sem)
+        read_query_ids()
         for n, (to, column) in enumerate(((y_right, 1), (y_left, 3), (y_far, 2))):
-            push(raw.at[0], raw.at[column], raw_send_sem.at[2 + n], raw_y_sem.at[n], (me, to))
+            push(key_ids.at[0], key_ids.at[column], raw_send_sem.at[2 + n], raw_y_sem.at[n], (me, to))
 
     def read_ids(column):
         parts = []
@@ -191,7 +192,7 @@
         chosen = jnp.where(mine & (ranks == slot_rank), value, 0.0).astype(BF16)
         key_ids[column] = lax.dot_general(
             jnp.ones((8, rows), BF16), chosen, (((1,), (1,)), ((), ())), preferred_element_type=F32
-        ) - 1.0
+        )[0:1] - 1.0
         return chosen
 
     strip = min(128, owners * 2 * CAP)
@@ -225,7 +226,7 @@
     best = [jnp.full((block, 1), LOWEST, F32) for _ in range(blocks)]
     query = []
 
-    def read_all_ids():
+    def read_query_ids():
         chosen = read_ids(0)
         query_id = jnp.dot(chosen, jnp.ones((rows, 128), BF16), preferred_element_type=F32)[:, 0:1] - 1.0
         query_temp = jnp.ones_like(query_id)
@@ -233,9 +234,10 @@
             query_temp = jnp.where(query_id == float(c), temp_ref[c], query_temp)
         query.append(jnp.where(query_id < 0.0, -2.0, query_id))
         query.append(query_temp)
+
+    def wait_ids():
         for n, column in enumerate((1, 3, 2)):
-            wait_bytes(raw.at[column], raw_y_sem.at[n])
-            read_ids(column)
+            wait_bytes(key_ids.at[column], raw_y_sem.at[n])
 
     def score(column, first, count, which):
         query_id, query_temp = query
@@ -282,7 +284,7 @@
         if m >= 2:
             far(m - 2)
         if m == min(5, NZ - 1):
-            read_all_ids()
+            wait_ids()
         if m == NZ - 1:
             score(0, 0, slots, every)
     relay(NZ - 1)
@@ -382,7 +384,7 @@
     wait_bytes(raw.at[0, pl.ds(1, NZ - 1), 0], raw_send_sem.at[0])
     wait_bytes(raw.at[0, :, pl.ds(1, group - 1)], raw_send_sem.at[1])
     for n in range(3):
-        wait_bytes(raw.at[0], raw_send_sem.at[2 + n])
+        wait_bytes(key_ids.at[0], raw_send_sem.at[2 + n])
     for way in range(2):
         wait_bytes(keys.at[0], y_send_sem.at[way])
         wait_bytes(keys.at[0, pl.ds(0, owners // 2)], relay_send_sem.at[way])
@@ -434,8 +436,8 @@
             pltpu.VMEM((owners, 2 * CAP, half), BF16),
             pltpu.VMEM((owners, 2 * CAP, half), BF16),
             pltpu.VMEM((2 * rows, owners * 2 * CAP), BF16),
-            pltpu.VMEM((NY, NZ, group, 1, rows), jnp.int32),
-            pltpu.VMEM((NY, 8, slots), F32),
+            pltpu.VMEM((1, NZ, group, 1, rows), jnp.int32),
+            pltpu.VMEM((NY, 1, slots), F32),
             pltpu.VMEM((NZ, group, 1, 128), F32),
             pltpu.VMEM((NZ, group, 1, 128), F32),
             pltpu.VMEM((NZ, group, 1, 128), F32),

time: 81.3 us -> 80.2 us (0.986)
  Pallas kernels: 79.2 us -> 78.2 us
    pallas_call x1, Pallas kernels: 79.2 us -> 78.2 us  [per_device(): pl.pallas_call(kernel, out_shape=(jax.ShapeDtypeStruct((rows, width), F32...]
where the time goes in v5:
time: 80.2 us; the launch traced here: 80.1 us
  Pallas kernels  78.2 us (98%)
  local copies, waits for them, and re-layouts  1.31 us (2%)
    pallas_call x1, Pallas kernels, per_device(): pl.pallas_call(kernel, out_shape=(jax.ShapeDtypeStruct((rows, width), F32...  78.2 us

profile of v5, /device:TPU:1, one launch (start us, length us, event | category | flops | bytes accessed | tf_op | source)
XLA Modules:
  0.0 80.1 jit_solution(1970962683970147490)
XLA Ops:
  0.6 78.2 %shard_map.50 = (f32[128,1024]{1,0:T(8,128)S(1)}, f32[1,128]{1,0:T(1,128)S(1)}) custom-call(s32[1,128]{1,0:T(1,128)} %bitcast.3, f32[128,1024]{1,0:T(8,128)} %x_hbm.1, f32[4]{0:T(128)} %temp_hbm.1), custom_call_target="tpu_custom_call" | custom-call | tf_op jit(solution)/shard_map/pallas_call | solution.py:420
  78.8 0.8 copy.7
  79.6 0.5 copy.8
